TPU v7x, 512 devices: a whole 4x4x16 slice. The times are simulated.
512 devices in a mesh: ctx: 32 (over x, y, core), head: 16 (over z).
Axes of the slice: x: 4, y: 4, z: 16, core: 2. Of those that a mesh axis runs over, the one named last changes fastest.
Arguments:
- tokens: bfloat16 [4096, 4096], P('ctx', 'head'), may hold values from -6 to 6
- w_query: bfloat16 [4096, 2048], P(None, 'head'), may hold values from -0.09375 to 0.09375
- w_key: bfloat16 [4096, 2048], P(None, 'head'), may hold values from -0.09375 to 0.09375
- w_value: bfloat16 [4096, 2048], P(None, 'head'), may hold values from -0.09375 to 0.09375
- w_beta: bfloat16 [4096, 16], P(None, 'head'), may hold values from -0.046875 to 0.046875
- beta_bias: float32 [16], P('head'), may hold values from -4.6 to 2, as said below
- w_out: bfloat16 [2048, 4096], P('head'), may hold values from -0.125 to 0.125
Outputs:
- mixed_out: bfloat16 [4096, 4096], P('ctx', 'head')
Inputs may be any that keep to these rules, and one draw needn't show every extreme that they name: `beta_bias`: one bias for each head.
All inputs are finite; a program needn't handle non-finite values.
Results may differ from a plain program's by a relative error of at most 0.025.
Values may be sent and summed in bfloat16 or wider, within the bound.
A program may use at most 64 MiB of HBM per device.

v0:
```python
import jax
import jax.numpy as jnp
from jax import lax
from jax.sharding import PartitionSpec as P

SPAN = 128


highest = lax.Precision.HIGHEST


def prefix_2(shard, axis, join, neutral):
    place = lax.axis_index(axis)
    gathered = jax.tree.map(
        lambda a, kind: lax.all_gather(a.astype(kind), axis), shard, (jnp.bfloat16, jnp.bfloat16)
    )
    state = jax.tree.map(lambda a, e: jnp.zeros_like(a) + jnp.asarray(e, a.dtype), shard, neutral)

    def one(step, state):
        return join(
            state,
            jax.tree.map(
                lambda a, own: lax.dynamic_index_in_dim(a, step, 0, False).astype(own.dtype),
                gathered,
                shard,
            ),
        )

    return lax.fori_loop(0, place, one, state)


def unit_rows(matrix):
    return matrix / jnp.sqrt(jnp.sum(matrix * matrix, axis=-1, keepdims=True) + 1e-06)


def lower_solve(system, right_side):
    return lax.linalg.triangular_solve(
        system, right_side, left_side=True, lower=True, unit_diagonal=True
    )


def apply_pair(trans, states, target):
    return jnp.einsum("hij,hjk->hik", trans, target, precision=highest) + states


def combine(earlier, later):
    trans = jnp.einsum("hij,hjk->hik", later[0], earlier[0], precision=highest)
    states = apply_pair(later[0], later[1], earlier[1])
    return (trans, states)


def shards(tokens, w_query, w_key, w_value, w_beta, beta_bias, w_out):
    tok_rows = tokens.shape[0]
    head_count = beta_bias.shape[0]
    key_width = w_key.shape[1] // head_count
    value_width = w_value.shape[1] // head_count
    block_count = tok_rows // SPAN
    weights = (w_query, w_key, w_value, w_beta)
    piece = lax.all_gather(tokens, "head", axis=1, tiled=True)
    query, key_all, value, beta = tuple(
        (jnp.dot(piece, weight, preferred_element_type=jnp.float32) for weight in weights)
    )

    def blocked(matrix, width):
        return matrix.reshape(block_count, SPAN, head_count, width).transpose(2, 0, 1, 3)

    query = blocked(unit_rows(query.reshape(tok_rows, head_count, key_width)), key_width)
    key_all = blocked(unit_rows(key_all.reshape(tok_rows, head_count, key_width)), key_width)
    value = blocked(value, value_width)
    beta = (
        jax.nn.sigmoid(beta + beta_bias).reshape(block_count, SPAN, head_count).transpose(2, 0, 1)
    )
    strict = jnp.tril(jnp.ones((SPAN, SPAN), jnp.float32), -1)
    causal_mask = jnp.tril(jnp.ones((SPAN, SPAN), jnp.float32))
    inner = jnp.einsum("hnid,hnjd->hnij", key_all, key_all, precision=highest)
    system = jnp.eye(SPAN, dtype=jnp.float32) + strict * beta[..., :, None] * inner
    weighted = lower_solve(system, beta[..., None] * key_all)
    updates = lower_solve(system, beta[..., None] * value)
    causal = causal_mask * jnp.einsum("hnid,hnjd->hnij", query, key_all, precision=highest)
    local_out = jnp.einsum("hnij,hnje->hnie", causal, updates, precision=highest)
    reader = query - jnp.einsum("hnij,hnjd->hnid", causal, weighted, precision=highest)
    block_trans = jnp.eye(key_width, dtype=jnp.float32) - jnp.einsum(
        "hnid,hnie->hnde", key_all, weighted, precision=highest
    )
    block_states = jnp.einsum("hnid,hnie->hnde", key_all, updates, precision=highest)
    run_trans = jnp.broadcast_to(
        jnp.eye(key_width, dtype=jnp.float32), (head_count, key_width, key_width)
    )
    run_states = jnp.zeros((head_count, key_width, value_width), jnp.float32)
    readers = []
    bases = []
    readers.append(jnp.einsum("hcd,hde->hce", reader[:, 0], run_trans, precision=highest))
    bases.append(
        local_out[:, 0] + jnp.einsum("hcd,hde->hce", reader[:, 0], run_states, precision=highest)
    )
    run_states = apply_pair(block_trans[:, 0], block_states[:, 0], run_states)
    run_trans = jnp.einsum("hij,hjk->hik", block_trans[:, 0], run_trans, precision=highest)
    readers = jnp.stack(readers, axis=1)
    bases = jnp.stack(bases, axis=1)
    identity = (
        jnp.broadcast_to(jnp.eye(key_width, dtype=jnp.float32), run_trans.shape),
        jnp.zeros_like(run_states),
    )
    prefix = prefix_2((run_trans, run_states), "ctx", combine, identity)
    entry_state = prefix[1]
    attended = bases + jnp.einsum("hncd,hde->hnce", readers, entry_state, precision=highest)
    attended = (
        attended.transpose(1, 2, 0, 3)
        .reshape(tok_rows, head_count * value_width)
        .astype(jnp.bfloat16)
    )
    terms = jnp.dot(attended, w_out, preferred_element_type=jnp.float32)
    return lax.psum_scatter(terms.astype(jnp.bfloat16), "head", scatter_dimension=1, tiled=True)


def solution(mesh):
    in_specs = (
        P("ctx", "head"),
        P(None, "head"),
        P(None, "head"),
        P(None, "head"),
        P(None, "head"),
        P("head"),
        P("head", None),
    )
    out_specs = P("ctx", "head")
    return jax.shard_map(shards, mesh=mesh, in_specs=in_specs, out_specs=out_specs, check_vma=False)
```

profile of v0, /device:TPU:6, one launch (start us, length us, event | category | flops | bytes accessed | tf_op | source)
XLA Modules:
  0.0 325.4 jit_solution(11446159685441483406)
XLA Ops:
  8.0 78.1 %all-gather.6.cloned.1.call-done = bf16[128,4096]{1,0:T(8,128)(2,1)} async-done(((bf16[128,256]{1,0:T(8,128)(2,1)}), bf16[128,4096]{1,0:T(8,128)(2,1)}) %all-gather.6.cloned.1.call-update) | async-done | bytes 1048592 | tf_op jit(solution)/shard_map/all_gather | solution.py:59
  86.1 2.2 multiply_reduce_fusion
  89.8 9.8 %custom-call.4 = f32[1,1,1,128,128]{3,4,2,1,0:T(8,128)S(1)} custom-call(f32[1,1,1,128,128]{4,3,2,1,0:T(8,128)S(1)} %fusion.11), custom_call_target="InvertDiagBlocksLowerTriangular" | custom-call | tf_op jit(solution)/shard_map/triangular_solve/custom-call.1 | solution.py:37
  101.3 1.0 fusion.7
  104.6 51.4 %all-gather.10.cloned.1.call-done = bf16[4096,128]{1,0:T(8,128)(2,1)} async-done(((bf16[128,128]{1,0:T(8,128)(2,1)}), bf16[4096,128]{1,0:T(8,128)(2,1)}) %all-gather.10.cloned.1.call-update) | async-done | bytes 1048592 | tf_op jit(solution)/shard_map/all_gather | solution.py:15
  156.0 60.7 %all-gather.8.cloned.1.call-done = bf16[4096,128]{1,0:T(8,128)(2,1)} async-done(((bf16[128,128]{1,0:T(8,128)(2,1)}), bf16[4096,128]{1,0:T(8,128)(2,1)}) %all-gather.8.cloned.1.call-update) | async-done | bytes 1048592 | tf_op jit(solution)/shard_map/all_gather | solution.py:15
  216.7 24.0 %while.12 = (s32[]{:T(128)}, f32[1,128,128]{2,1,0:T(8,128)S(1)}, s32[]{:T(128)}, bf16[32,1,128,128]{3,2,1,0:T(8,128)(2,1)}, bf16[32,1,128,128]{3,2,1,0:T(8,128)(2,1)}, /*index=5*/s32[]{:T(128)}, s32[]{:T(128)}, s32[]{:T(128)}) while((s32[]{:T(128)}, f32[1,128,128]{2,1,0:T(8,128)S(1)}, s32[]{:T(128)}, bf16[32,1,128,128]{3,2,1,0:T(8,128)(2,1)}, ...), condition=%wide.region_3.5_spmd, body=%wide.region_2.4_spmd.sunk | while | flops 25198596 | bytes 328831 | solution.py:29
  216.8 1.0 fusion.58
  217.8 1.0 fusion.58
  218.8 1.0 fusion.58
  219.8 1.0 fusion.58
  220.8 1.0 fusion.58
  221.8 1.0 fusion.58
  222.8 1.0 fusion.58
  223.8 1.0 fusion.58
  224.8 1.0 fusion.58
  225.8 1.0 fusion.58
  226.8 1.0 fusion.58
  230.8 1.0 fusion.58
  233.8 1.0 fusion.58
  234.8 1.0 fusion.58
  237.8 1.0 fusion.58
  241.0 1.4 convolution_convert_fusion
  242.4 76.4 %reduce-scatter.2.cloned.1.call-done = bf16[128,256]{1,0:T(8,128)(2,1)} async-done(((bf16[128,4096]{1,0:T(8,128)(2,1)}), bf16[128,256]{1,0:T(8,128)(2,1)}) %reduce-scatter.2.cloned.1.call-update) | async-done | bytes 65552 | tf_op jit(solution)/shard_map/reduce_scatter | solution.py:113
  (70 shorter events, 15.2 us)
Async XLA Ops:
  6.5 234.5 %copy-start = (bf16[128,4096]{1,0:T(8,128)(2,1)S(1)}, bf16[128,4096]{1,0:T(8,128)(2,1)}, u32[]{:S(2)}) copy-start(bf16[128,4096]{1,0:T(8,128)(2,1)} %param.17) | copy-start | bytes 3145732
  6.5 79.5 %all-gather.6.cloned.1.call-start = ((), (), s32[]{:S(2)}) async-start(), calls=%async_computation.1 | async-start | bytes 1114112 | tf_op jit(solution)/shard_map/all_gather | solution.py:59
  7.3 148.8 %all-gather.10.cloned.1.call-start = ((), (), s32[]{:S(2)}) async-start(), calls=%async_computation.4 | async-start | bytes 1081344 | tf_op jit(solution)/shard_map/all_gather | solution.py:15
  8.0 80.4 %copy-start.2 = (bf16[4096,128]{1,0:T(8,128)(2,1)S(1)}, bf16[4096,128]{1,0:T(8,128)(2,1)}, u32[]{:S(2)}) copy-start(bf16[4096,128]{1,0:T(8,128)(2,1)} %param.12) | copy-start | bytes 3145732
  86.1 2.3 copy-start.1
  88.4 0.7 copy-start.4
  88.9 11.1 %copy-start.3 = (bf16[4096,128]{1,0:T(8,128)(2,1)S(1)}, bf16[4096,128]{1,0:T(8,128)(2,1)}, u32[]{:S(2)}) copy-start(bf16[4096,128]{1,0:T(8,128)(2,1)} %param.14) | copy-start | bytes 3145732
  102.3 114.5 %all-gather.8.cloned.1.call-start = ((), (), s32[]{:S(2)}) async-start(), calls=%async_computation.3 | async-start | bytes 1081344 | tf_op jit(solution)/shard_map/all_gather | solution.py:15
  103.2 215.7 %reduce-scatter.2.cloned.1.call-start = ((), (), s32[]{:S(2)}) async-start(), calls=%async_computation.2 | async-start | bytes 1114112 | tf_op jit(solution)/shard_map/reduce_scatter | solution.py:113
Sparse Core Ops, SparseCore 0:
  9.4 76.6 all-gather.5
  102.4 53.5 all-gather.9
  159.2 57.5 all-gather.7
  242.6 76.2 reduce-scatter.1
where the time goes:
time: 328 us; the launch traced here: 325 us
  waiting for transfers between devices  267 us (81%)
  matrix products  32.8 us (10%)
  between operations  14 us (4%)
  other arithmetic  9.82 us (3%)
    all_gather x2, waiting for transfers between devices, prefix_2(): lax.all_gather(a.astype(kind), axis)  112 us
    all_gather x1, waiting for transfers between devices, shards(): piece = lax.all_gather(tokens, 'head', axis=1, tiled=True)  78.1 us
    reduce_scatter x1, waiting for transfers between devices, shards(): lax.psum_scatter(terms.astype(jnp.bfloat16), 'head', scatter_dimension=1,...  76.4 us
    dot_general x25, matrix products, apply_pair(): return jnp.einsum('hij,hjk->hik', trans, target, precision=highest) + states  23.2 us
    another operation x2, other arithmetic, lower_solve(): lax.linalg.triangular_solve(system, right_side, left_side=True, lower=Tru...  9.81 us
  transfers between devices with their start and end apart: 4, of which 4 were waited for; matrix products, arithmetic and copies ran while one was open for 1% of the time, Pallas kernels for 0%

commit v1 on v0

v1 whole, which is shorter than its diff:
```python
import functools

import jax
import jax.numpy as jnp
from jax import lax
from jax.experimental import pallas as pl
from jax.experimental.pallas import tpu as pltpu
from jax.sharding import PartitionSpec as P

MESH = pl.DeviceIdType.MESH
BF = jnp.bfloat16
F32 = jnp.float32
NZ = 16
CHIPS = 16
YS = 4
XS = 4
ROWS = 128
FEAT = 256
DK = 128
LAG = 6


def tree_step2():
    parent = {}
    for s in (1, -1):
        parent.update({2 * s: 0, 4 * s: 2 * s, 6 * s: 4 * s, s: 0, 3 * s: 2 * s, 5 * s: 4 * s, 7 * s: 6 * s})
    parent[8] = 6
    return [2, -2, 1, -1, 4, -4, 3, -3, 6, -6, 5, -5, 8, 7, -7], parent


def tree_step3():
    parent = {3: 0, -3: 0, 6: 3, -6: -3, 8: 6}
    for s in (0, 3, -3, 6, -6):
        parent[s + 1] = s
        parent[s - 1] = s
    return [3, -3, 1, -1, 6, -6, 4, -4, 2, -2, 5, -5, 7, -7, 8], parent


TREE_A = tree_step2()
TREE_D = tree_step3()


def split(a):
    high = a.astype(BF)
    return high, (a - high.astype(F32)).astype(BF)


def dot(a, b):
    return jnp.dot(a, b, preferred_element_type=F32)


def dot_nt(a, b):
    return lax.dot_general(a, b, (((1,), (1,)), ((), ())), preferred_element_type=F32)


def dot_tn(a, b):
    return lax.dot_general(a, b, (((0,), (0,)), ((), ())), preferred_element_type=F32)


def three(product, a, b):
    ah, al = a
    bh, bl = b
    return product(ah, bh) + (product(ah, bl) + product(al, bh))


def mm3(a, b):
    return three(dot, split(a), split(b))


def mm2(n, s):
    high, low = split(s)
    return dot(n, high) + dot(n, low)


def lower_inverse(low):
    r = lax.broadcasted_iota(jnp.int32, (ROWS, ROWS), 0)
    c = lax.broadcasted_iota(jnp.int32, (ROWS, ROWS), 1)
    b = 16
    count = ROWS // b
    diag = jnp.where((r // b) == (c // b), low, 0.0)
    x = (r == c).astype(F32).reshape(count, b, ROWS)
    for j in range(b - 1):
        col = jnp.sum(jnp.where((c % b) == j, diag, 0.0), axis=1, keepdims=True)
        x = x - col.reshape(count, b, 1) * x[:, j : j + 1, :]
    x = x.reshape(ROWS, ROWS)
    w = b
    while w < ROWS:
        off = jnp.where(((r // w) % 2 == 1) & ((c // w) == (r // w) - 1), low, 0.0)
        x = x - mm3(x, mm3(off, x))
        w *= 2
    return x


def kernel(
    tokens, w_query, w_key, w_value, w_beta, bias, w_out, out,
    own, tok, weights, wb32, acc, accb, wo, own_x, peer_x, total, chain, state, att_own, att,
    reader_s, local_s,
    load_sem, w_sem, a_send, a_recv, w1_send, w1_recv, w1_own, w2_send, w2_recv, w3_send, w3_recv,
    c_send, c_recv, p_send, p_recv, f_send, f_recv, d_send, d_recv, hello,
):
    z = lax.axis_index("head")
    ctx = lax.axis_index("ctx")
    core = lax.rem(ctx, 2)
    chip = ctx // 2
    x = chip // YS
    y = lax.rem(chip, YS)
    peer = ctx + 1 - 2 * core

    def head_at(off):
        return lax.rem(z + (off + 2 * NZ) % NZ, NZ)

    load = pltpu.make_async_copy(tokens, own, load_sem)
    load.start()
    w_loads = [
        pltpu.make_async_copy(w, weights.at[:, pl.ds(DK * i, DK)], w_sem.at[i])
        for i, w in enumerate((w_query, w_key, w_value))
    ]
    for w in w_loads:
        w.start()

    x_peers = [(lax.rem(x + d, XS) * YS + y) * 2 + core for d in (1, 2, 3)]
    y_peers = [(x * YS + lax.rem(y + d, YS)) * 2 + core for d in (1, 2, 3)]
    z_offs = sorted({(o - TREE_A[1][o]) % NZ for o in TREE_A[0]} | {(TREE_A[1][o] - o) % NZ for o in TREE_A[0]})
    barrier = pltpu.get_barrier_semaphore()
    for off in z_offs:
        pl.semaphore_signal(barrier, inc=1, device_id={"head": head_at(off)}, device_id_type=MESH)
    for c in x_peers + y_peers + [peer]:
        pl.semaphore_signal(barrier, inc=1, device_id={"ctx": c}, device_id_type=MESH)
    pl.semaphore_wait(barrier, len(z_offs) + 7)

    def tree_copies(order, parent, first, slots, send, recv):
        def copy(o):
            p = parent[o]
            return pltpu.make_async_remote_copy(
                src_ref=first if p == 0 else slots.at[p % NZ],
                dst_ref=slots.at[o % NZ],
                send_sem=send.at[o % NZ],
                recv_sem=recv.at[o % NZ],
                device_id={"head": head_at(o - p)},
                device_id_type=MESH,
            )

        kids = {}
        for o in order:
            kids.setdefault(parent[o], []).append(o)
        return copy, kids

    order_a, parent_a = TREE_A
    a_copy, a_kids = tree_copies(order_a, parent_a, own, tok, a_send, a_recv)
    load.wait()
    for o in a_kids[0]:
        a_copy(o).start()
    for c in x_peers:
        pl.semaphore_signal(hello, inc=1, device_id={"ctx": c}, device_id_type=MESH)

    row_tile = pl.multiple_of((chip // 2) * 16, 16)
    col_tile = pl.multiple_of(lax.rem(chip, 2) * 128, 128)
    half = lax.rem(core + z, 2)

    def tile_of(parity, index):
        return wo.at[parity, index, pl.ds(row_tile, 16), pl.ds(col_tile, 128)]

    def w1_copy(off):
        target = head_at(-off)
        return pltpu.make_async_remote_copy(
            src_ref=w_out.at[
                pl.ds(row_tile, 16), pl.ds(pl.multiple_of(target * FEAT + col_tile, 128), 128)
            ],
            dst_ref=tile_of(lax.rem(z, 2), z // 2),
            send_sem=w1_send.at[off % NZ],
            recv_sem=w1_recv.at[(-off) % NZ],
            device_id={"head": target},
            device_id_type=MESH,
        )

    w1_mine = pltpu.make_async_copy(
        w_out.at[pl.ds(row_tile, 16), pl.ds(pl.multiple_of(z * FEAT + col_tile, 128), 128)],
        tile_of(lax.rem(z, 2), z // 2),
        w1_own,
    )

    @pl.when(core == 0)
    def _():
        w1_mine.start()

    for w in w_loads:
        w.wait()
    for i in range(NZ):
        wb32[i : i + 1, :] = w_beta[:, i * FEAT : (i + 1) * FEAT].astype(F32)

    def project(block, off, first):
        owner = head_at(-off)
        rows = pl.ds(pl.multiple_of(owner * FEAT, FEAT), FEAT)
        part = dot(block, weights[rows, :])
        beta = block.astype(F32) * wb32[pl.ds(owner, 1), :]
        if first:
            acc[...] = part
            accb[...] = beta
        else:
            acc[...] += part
            accb[...] += beta

    project(own[...], 0, True)
    for o in order_a:
        a_copy(o).wait_recv()
        for q in a_kids.get(o, ()):
            a_copy(q).start()

        @pl.when(core == o % 2)
        def _():
            w1_copy(o).start()

        project(tok[o % NZ], o, False)

    def unit(m):
        return m / jnp.sqrt(jnp.sum(m * m, axis=1, keepdims=True) + 1e-06)

    query = unit(acc[:, 0:DK])
    key = unit(acc[:, DK : 2 * DK])
    value = acc[:, 2 * DK : 3 * DK]
    beta = jax.nn.sigmoid(jnp.sum(accb[...], axis=1, keepdims=True) + bias[0])
    r = lax.broadcasted_iota(jnp.int32, (ROWS, ROWS), 0)
    c = lax.broadcasted_iota(jnp.int32, (ROWS, ROWS), 1)
    key2 = split(key)
    inner = three(dot_nt, key2, key2)
    inverse = lower_inverse(jnp.where(r > c, beta * inner, 0.0))
    solved = mm3(inverse, jnp.concatenate([beta * key, beta * value], axis=1))
    solved2 = split(solved)
    mine = three(dot_tn, key2, solved2)
    own_x[...] = mine.astype(BF)
    c_copy = pltpu.make_async_remote_copy(
        src_ref=own_x, dst_ref=peer_x, send_sem=c_send, recv_sem=c_recv,
        device_id={"ctx": peer}, device_id_type=MESH,
    )
    c_copy.start()
    causal = jnp.where(r >= c, three(dot_nt, split(query), key2), 0.0)
    seen = three(dot, split(causal), solved2)
    reader_s[...] = query - seen[:, 0:DK]
    local_s[...] = seen[:, DK:]
    c_copy.wait_recv()
    other = peer_x[...].astype(F32)
    early = jnp.where(core == 0, mine, other)
    late = jnp.where(core == 0, other, mine)
    total[...] = (early + late - mm3(late[:, 0:DK], early)).astype(BF)

    mine_rows = pl.ds(pl.multiple_of(core * 64, 64), 64)
    pl.semaphore_wait(hello, 3)

    def p_copy(target):
        return pltpu.make_async_remote_copy(
            src_ref=total.at[mine_rows], dst_ref=chain.at[chip, mine_rows],
            send_sem=p_send.at[target], recv_sem=p_recv.at[chip],
            device_id={"ctx": target * 2 + core}, device_id_type=MESH,
        )

    def p_arrival(source):
        return pltpu.make_async_remote_copy(
            src_ref=total.at[mine_rows], dst_ref=chain.at[source, mine_rows],
            send_sem=p_send.at[source], recv_sem=p_recv.at[source],
            device_id={"ctx": source * 2 + core}, device_id_type=MESH,
        )

    def f_copy(source):
        return pltpu.make_async_remote_copy(
            src_ref=chain.at[source, mine_rows], dst_ref=chain.at[source, mine_rows],
            send_sem=f_send.at[source], recv_sem=f_recv.at[source],
            device_id={"ctx": peer}, device_id_type=MESH,
        )

    @pl.loop(0, CHIPS - 1)
    def _(i):
        target = CHIPS - 1 - i

        @pl.when(target > chip)
        def _():
            p_copy(target).start()

    for o in range(NZ):

        @pl.when(core == o % 2)
        def _():
            if o == 0:
                w1_mine.wait()
            else:
                w1_copy(-o).wait_recv()

    def w2_copy(d):
        target = lax.rem(chip + d, CHIPS)
        tiles = wo.at[half, :, pl.ds(row_tile, 16), pl.ds(col_tile, 128)]
        return pltpu.make_async_remote_copy(
            src_ref=tiles, dst_ref=tiles,
            send_sem=w2_send.at[d], recv_sem=w2_recv.at[d],
            device_id={"ctx": target * 2 + core}, device_id_type=MESH,
        )

    @pl.loop(1, CHIPS)
    def _(d):
        w2_copy(d).start()

    state[...] = jnp.zeros_like(state)

    @pl.loop(0, CHIPS - 1 + LAG)
    def _(t):
        @pl.when(t < chip)
        def _():
            p_arrival(t).wait_recv()
            f_copy(t).start()

        @pl.when((t >= LAG) & (t - LAG < chip))
        def _():
            s = t - LAG
            f_copy(s).wait_recv()
            step = chain[s]
            state[...] += step[:, DK:].astype(F32) - mm2(step[:, 0:DK], state[...])

    entry = state[...]
    moved = entry + peer_x[:, DK:].astype(F32) - mm2(peer_x[:, 0:DK], entry)
    entry = jnp.where(core == 0, entry, moved)
    att_own[...] = (local_s[...] + mm3(reader_s[...], entry)).astype(BF)

    order_d, parent_d = TREE_D
    d_copy, d_kids = tree_copies(order_d, parent_d, att_own, att, d_send, d_recv)
    for o in d_kids[0]:
        d_copy(o).start()

    def w2_arrival(d):
        source = lax.rem(chip + CHIPS - d, CHIPS)
        tiles = wo.at[
            half, :,
            pl.ds(pl.multiple_of((source // 2) * 16, 16), 16),
            pl.ds(pl.multiple_of(lax.rem(source, 2) * 128, 128), 128),
        ]
        return pltpu.make_async_remote_copy(
            src_ref=tiles, dst_ref=tiles,
            send_sem=w2_send.at[d], recv_sem=w2_recv.at[d],
            device_id={"ctx": source * 2 + core}, device_id_type=MESH,
        )

    @pl.loop(1, CHIPS)
    def _(d):
        w2_arrival(d).wait_recv()

    w3_copy = pltpu.make_async_remote_copy(
        src_ref=wo.at[half], dst_ref=wo.at[half], send_sem=w3_send, recv_sem=w3_recv,
        device_id={"ctx": peer}, device_id_type=MESH,
    )
    w3_copy.start()
    w3_arrival = pltpu.make_async_remote_copy(
        src_ref=wo.at[1 - half], dst_ref=wo.at[1 - half], send_sem=w3_send, recv_sem=w3_recv,
        device_id={"ctx": peer}, device_id_type=MESH,
    )
    w3_arrival.wait_recv()

    def columns(off):
        owner = head_at(-off)
        return wo[lax.rem(owner, 2), owner // 2]

    result = dot(att_own[...], columns(0))
    for o in order_d:
        d_copy(o).wait_recv()
        for q in d_kids.get(o, ()):
            d_copy(q).start()
        result = result + dot(att[o % NZ], columns(o))
    out[...] = result.astype(BF)

    for o in order_a:
        a_copy(o).wait_send()

        @pl.when(core == o % 2)
        def _():
            w1_copy(o).wait_send()

    c_copy.wait_send()

    @pl.loop(0, CHIPS)
    def _(i):
        @pl.when(i > chip)
        def _():
            p_copy(i).wait_send()

        @pl.when(i < chip)
        def _():
            f_copy(i).wait_send()

        @pl.when(i > 0)
        def _():
            w2_copy(i).wait_send()

    w3_copy.wait_send()
    for o in order_d:
        d_copy(o).wait_send()


def shards(tokens, w_query, w_key, w_value, w_beta, beta_bias, w_out):
    hbm = pl.BlockSpec(memory_space=pltpu.HBM)
    vmem = pl.BlockSpec(memory_space=pltpu.VMEM)
    smem = pl.BlockSpec(memory_space=pltpu.SMEM)
    dma = pltpu.SemaphoreType.DMA
    return pl.pallas_call(
        kernel,
        out_shape=jax.ShapeDtypeStruct((ROWS, FEAT), BF),
        in_specs=[hbm, hbm, hbm, hbm, vmem, smem, hbm],
        out_specs=vmem,
        scratch_shapes=[
            pltpu.VMEM((ROWS, FEAT), BF),
            pltpu.VMEM((NZ, ROWS, FEAT), BF),
            pltpu.VMEM((NZ * FEAT, 3 * DK), BF),
            pltpu.VMEM((NZ, FEAT), F32),
            pltpu.VMEM((ROWS, 3 * DK), F32),
            pltpu.VMEM((ROWS, FEAT), F32),
            pltpu.VMEM((2, NZ // 2, ROWS, FEAT), BF),
            pltpu.VMEM((ROWS, 2 * DK), BF),
            pltpu.VMEM((ROWS, 2 * DK), BF),
            pltpu.VMEM((ROWS, 2 * DK), BF),
            pltpu.VMEM((CHIPS, ROWS, 2 * DK), BF),
            pltpu.VMEM((DK, DK), F32),
            pltpu.VMEM((ROWS, DK), BF),
            pltpu.VMEM((NZ, ROWS, DK), BF),
            pltpu.VMEM((ROWS, DK), F32),
            pltpu.VMEM((ROWS, DK), F32),
            dma, dma((3,)), dma((NZ,)), dma((NZ,)),
            dma((NZ,)), dma((NZ,)), dma, dma((CHIPS,)), dma((CHIPS,)), dma, dma,
            dma, dma, dma((CHIPS,)), dma((CHIPS,)), dma((CHIPS,)), dma((CHIPS,)),
            dma((NZ,)), dma((NZ,)), pltpu.SemaphoreType.REGULAR,
        ],
        compiler_params=pltpu.CompilerParams(
            collective_id=0, has_side_effects=True, vmem_limit_bytes=63 * 2**20
        ),
    )(tokens, w_query, w_key, w_value, w_beta.T, beta_bias, w_out)


def solution(mesh):
    in_specs = (
        P("ctx", "head"),
        P(None, "head"),
        P(None, "head"),
        P(None, "head"),
        P(None, "head"),
        P("head"),
        P("head", None),
    )
    return jax.shard_map(
        shards, mesh=mesh, in_specs=in_specs, out_specs=P("ctx", "head"), check_vma=False
    )
```

time: 328 us -> 72.2 us (0.22)
  waiting for transfers between devices: 267 us -> 0 us
  Pallas kernels: 0 us -> 69.9 us
  matrix products: 32.8 us -> 0 us
  between operations: 14 us -> 0.66 us
  other arithmetic: 9.82 us -> 0 us
    all_gather x3 -> x0, waiting for transfers between devices: 190 us -> none  [the longest x2 112 us: prefix_2(): lax.all_gather(a.astype(kind), axis)]
    reduce_scatter x1 -> x0, waiting for transfers between devices: 76.4 us -> none  [shards(): lax.psum_scatter(terms.astype(jnp.bfloat16), 'head', scatter_dimension=1,...]
    pallas_call x0 -> x1, Pallas kernels: none -> 69.9 us  [shards(): pl.pallas_call(kernel, out_shape=jax.ShapeDtypeStruct((ROWS, FEAT), BF),...]
    dot_general x40 -> x0, matrix products: 32.2 us -> none  [the longest x25 23.2 us: apply_pair(): return jnp.einsum('hij,hjk->hik', trans, target, precision=highest) + states]
    another operation x2 -> x0, other arithmetic: 9.81 us -> none  [lower_solve(): lax.linalg.triangular_solve(system, right_side, left_side=True, lower=Tru...]
  transfers between devices with their start and end apart: 4 -> 0, of which waited for: 4 -> 0; matrix products, arithmetic and copies ran while one was open for 1% -> 0% of each run, Pallas kernels for 0% -> 0%
where the time goes in v1:
time: 72.2 us; the launch traced here: 72 us
  Pallas kernels  69.9 us (97%)
  local copies, waits for them, and re-layouts  1.47 us (2%)
    pallas_call x1, Pallas kernels, shards(): pl.pallas_call(kernel, out_shape=jax.ShapeDtypeStruct((ROWS, FEAT), BF),...  69.9 us
    unnamed x1, local copies, waits for them, and re-layouts  1.47 us

profile of v1, /device:TPU:6, one launch (start us, length us, event | category | flops | bytes accessed | tf_op | source)
XLA Modules:
  0.0 72.0 jit_solution(6409362971810691254)
XLA Ops:
  0.7 69.9 %shard_map.73 = bf16[128,256]{1,0:T(8,128)(2,1)} custom-call(bf16[128,256]{1,0:T(8,128)(2,1)} %tokens.1, bf16[4096,128]{1,0:T(8,128)(2,1)} %w_query.1, bf16[4096,128]{1,0:T(8,128)(2,1)} %w_key.1, bf16[4096,128]{1,0:T(8,128)(2,1)} %w_value.1, bf16[1,4096]{1,0:T(2,128)(2,1)} %bitcast.1, f32[1]{0:T(128)S(6)} %copy.9.bias, bf16[128,4096]{1,0:T(8,128)(2,1)} %w_out.1), custom_call_target="tpu_custom_call" | custom-call | tf_op jit(solution)/shard_map/pallas_call | solution.py:399
  70.6 1.5 %copy.10 = bf16[128,256]{1,0:T(8,128)(2,1)} copy(bf16[128,256]{1,0:T(8,128)(2,1)} %shard_map.73) | data formatting | bytes 131072

commit v2 on v1

--- a/solution.py
+++ b/solution.py
@@ -17,27 +17,31 @@
 ROWS = 128
 FEAT = 256
 DK = 128
-LAG = 6
+LAG = 4
+W1_AT = 1
+W2_AT = 10
 
 
 def tree_step2():
     parent = {}
     for s in (1, -1):
-        parent.update({2 * s: 0, 4 * s: 2 * s, 6 * s: 4 * s, s: 0, 3 * s: 2 * s, 5 * s: 4 * s, 7 * s: 6 * s})
-    parent[8] = 6
-    return [2, -2, 1, -1, 4, -4, 3, -3, 6, -6, 5, -5, 8, 7, -7], parent
-
-
-def tree_step3():
-    parent = {3: 0, -3: 0, 6: 3, -6: -3, 8: 6}
-    for s in (0, 3, -3, 6, -6):
-        parent[s + 1] = s
-        parent[s - 1] = s
-    return [3, -3, 1, -1, 6, -6, 4, -4, 2, -2, 5, -5, 7, -7, 8], parent
+        parent.update({2 * s: 0, 4 * s: 2 * s, 6 * s: 4 * s, 8 * s: 6 * s})
+        parent.update({s: 0, 3 * s: 2 * s, 5 * s: 4 * s, 7 * s: 6 * s})
+    return [2, -2, 1, -1, 4, -4, 3, -3, 6, -6, 5, -5, 8, -8, 7, -7], parent
+
+
+def tree_seed5():
+    parent = {8: 5, -8: -5}
+    for s in (0, 5, -5):
+        if s:
+            parent[s] = 0
+        for e in (1, -1, 2, -2):
+            parent[s + e] = s
+    return [5, -5, 1, -1, 2, -2, 4, -4, 6, -6, 3, -3, 7, -7, 8, -8], parent
 
 
 TREE_A = tree_step2()
-TREE_D = tree_step3()
+TREE_D = tree_seed5()
 
 
 def split(a):
@@ -92,11 +96,11 @@
 
 
 def kernel(
-    tokens, w_query, w_key, w_value, w_beta, bias, w_out, out,
-    own, tok, weights, wb32, acc, accb, wo, own_x, peer_x, total, chain, state, att_own, att,
+    tokens, w_query, w_key, w_value, w_beta_in, bias_in, w_out, out,
+    w_beta, bias, own, tok, weights, wb32, acc, accb, wo, own_x, peer_x, total, chain, state, att_own, att,
     reader_s, local_s,
     load_sem, w_sem, a_send, a_recv, w1_send, w1_recv, w1_own, w2_send, w2_recv, w3_send, w3_recv,
-    c_send, c_recv, p_send, p_recv, f_send, f_recv, d_send, d_recv, hello,
+    c_send, c_recv, pf_send, p_recv, f_recv, d_send, d_recv, hello,
 ):
     z = lax.axis_index("head")
     ctx = lax.axis_index("ctx")
@@ -107,16 +111,7 @@
     peer = ctx + 1 - 2 * core
 
     def head_at(off):
-        return lax.rem(z + (off + 2 * NZ) % NZ, NZ)
-
-    load = pltpu.make_async_copy(tokens, own, load_sem)
-    load.start()
-    w_loads = [
-        pltpu.make_async_copy(w, weights.at[:, pl.ds(DK * i, DK)], w_sem.at[i])
-        for i, w in enumerate((w_query, w_key, w_value))
-    ]
-    for w in w_loads:
-        w.start()
+        return lax.rem(z + off % NZ, NZ)
 
     x_peers = [(lax.rem(x + d, XS) * YS + y) * 2 + core for d in (1, 2, 3)]
     y_peers = [(x * YS + lax.rem(y + d, YS)) * 2 + core for d in (1, 2, 3)]
@@ -126,32 +121,51 @@
         pl.semaphore_signal(barrier, inc=1, device_id={"head": head_at(off)}, device_id_type=MESH)
     for c in x_peers + y_peers + [peer]:
         pl.semaphore_signal(barrier, inc=1, device_id={"ctx": c}, device_id_type=MESH)
+
+    load = pltpu.make_async_copy(tokens, own, load_sem)
+    load.start()
+    for i, w in enumerate((w_query, w_key, w_value)):
+        pltpu.make_async_copy(w, weights.at[:, pl.ds(DK * i, DK)], w_sem.at[0]).start()
+    w_loads = [
+        pltpu.make_async_copy(weights, weights, w_sem.at[0]),
+        pltpu.make_async_copy(w_beta_in, w_beta, w_sem.at[1]),
+        pltpu.make_async_copy(bias_in, bias, w_sem.at[2]),
+    ]
+    for w in w_loads[1:]:
+        w.start()
     pl.semaphore_wait(barrier, len(z_offs) + 7)
 
-    def tree_copies(order, parent, first, slots, send, recv):
+    def tree_copies(tree, first, slots, send, recv):
+        order, parent = tree
+
         def copy(o):
             p = parent[o]
+            target = head_at(o - p)
+            if o in (8, -8):
+                rows = pl.ds(0 if o > 0 else ROWS // 2, ROWS // 2)
+            else:
+                rows = pl.ds(0, ROWS)
             return pltpu.make_async_remote_copy(
-                src_ref=first if p == 0 else slots.at[p % NZ],
-                dst_ref=slots.at[o % NZ],
-                send_sem=send.at[o % NZ],
-                recv_sem=recv.at[o % NZ],
-                device_id={"head": head_at(o - p)},
+                src_ref=first.at[rows] if p == 0 else slots.at[p % NZ, rows],
+                dst_ref=slots.at[o % NZ, rows],
+                send_sem=send,
+                recv_sem=recv.at[0 if o == -8 else o % NZ],
+                device_id={"head": target},
                 device_id_type=MESH,
             )
 
         kids = {}
         for o in order:
             kids.setdefault(parent[o], []).append(o)
-        return copy, kids
-
-    order_a, parent_a = TREE_A
-    a_copy, a_kids = tree_copies(order_a, parent_a, own, tok, a_send, a_recv)
-    load.wait()
+        return order, copy, kids
+
+    order_a, a_copy, a_kids = tree_copies(TREE_A, tokens, tok, a_send, a_recv)
     for o in a_kids[0]:
         a_copy(o).start()
     for c in x_peers:
-        pl.semaphore_signal(hello, inc=1, device_id={"ctx": c}, device_id_type=MESH)
+        pl.semaphore_signal(hello.at[0], inc=1, device_id={"ctx": c}, device_id_type=MESH)
+    for off in (2, -2):
+        pl.semaphore_signal(hello.at[1], inc=1, device_id={"head": head_at(off)}, device_id_type=MESH)
 
     row_tile = pl.multiple_of((chip // 2) * 16, 16)
     col_tile = pl.multiple_of(lax.rem(chip, 2) * 128, 128)
@@ -167,8 +181,8 @@
                 pl.ds(row_tile, 16), pl.ds(pl.multiple_of(target * FEAT + col_tile, 128), 128)
             ],
             dst_ref=tile_of(lax.rem(z, 2), z // 2),
-            send_sem=w1_send.at[off % NZ],
-            recv_sem=w1_recv.at[(-off) % NZ],
+            send_sem=w1_send,
+            recv_sem=w1_recv,
             device_id={"head": target},
             device_id_type=MESH,
         )
@@ -200,17 +214,60 @@
             acc[...] += part
             accb[...] += beta
 
+    def bytes_of(ref, send, recv):
+        return pltpu.make_async_remote_copy(
+            src_ref=ref, dst_ref=ref, send_sem=send, recv_sem=recv,
+            device_id={"ctx": peer}, device_id_type=MESH,
+        )
+
+    w1_counts = (NZ // 2 - 1, NZ // 2)
+
+    def w1_bytes(count):
+        return bytes_of(wo.at[0, pl.ds(0, count), pl.ds(0, 16), pl.ds(0, 128)], w1_send, w1_recv)
+
+    w2_bytes = bytes_of(weights.at[pl.ds(0, 640)], w2_send, w2_recv)
+
+    def w2_copy(d):
+        target = lax.rem(chip + d, CHIPS)
+        tiles = wo.at[half, :, pl.ds(row_tile, 16), pl.ds(col_tile, 128)]
+        return pltpu.make_async_remote_copy(
+            src_ref=tiles, dst_ref=tiles, send_sem=w2_send, recv_sem=w2_recv,
+            device_id={"ctx": target * 2 + core}, device_id_type=MESH,
+        )
+
+    load.wait()
     project(own[...], 0, True)
-    for o in order_a:
+    pl.semaphore_wait(hello.at[1], 2)
+    for off in (4, -4):
+        pl.semaphore_signal(hello.at[2], inc=1, device_id={"head": head_at(off)}, device_id_type=MESH)
+    for step, o in enumerate(order_a):
         a_copy(o).wait_recv()
         for q in a_kids.get(o, ()):
             a_copy(q).start()
-
-        @pl.when(core == o % 2)
-        def _():
-            w1_copy(o).start()
-
-        project(tok[o % NZ], o, False)
+        if step == W1_AT:
+            pl.semaphore_wait(hello.at[2], 2)
+            for q in range(1, NZ):
+
+                @pl.when(core == q % 2)
+                def _():
+                    w1_copy(q).start()
+
+        if step == W2_AT:
+            pl.semaphore_wait(hello.at[0], 3)
+            for k in range(2):
+
+                @pl.when(core == k)
+                def _():
+                    w1_bytes(w1_counts[k]).wait_recv()
+                    if k == 0:
+                        w1_mine.wait()
+
+            @pl.loop(1, CHIPS)
+            def _(d):
+                w2_copy(d).start()
+
+        if o != 8:
+            project(tok[o % NZ], o, False)
 
     def unit(m):
         return m / jnp.sqrt(jnp.sum(m * m, axis=1, keepdims=True) + 1e-06)
@@ -241,29 +298,28 @@
     other = peer_x[...].astype(F32)
     early = jnp.where(core == 0, mine, other)
     late = jnp.where(core == 0, other, mine)
-    total[...] = (early + late - mm3(late[:, 0:DK], early)).astype(BF)
+    total[...] = (early + late - mm2(late[:, 0:DK].astype(BF), early)).astype(BF)
 
     mine_rows = pl.ds(pl.multiple_of(core * 64, 64), 64)
-    pl.semaphore_wait(hello, 3)
 
     def p_copy(target):
         return pltpu.make_async_remote_copy(
             src_ref=total.at[mine_rows], dst_ref=chain.at[chip, mine_rows],
-            send_sem=p_send.at[target], recv_sem=p_recv.at[chip],
+            send_sem=pf_send.at[target], recv_sem=p_recv.at[chip],
             device_id={"ctx": target * 2 + core}, device_id_type=MESH,
         )
 
     def p_arrival(source):
         return pltpu.make_async_remote_copy(
             src_ref=total.at[mine_rows], dst_ref=chain.at[source, mine_rows],
-            send_sem=p_send.at[source], recv_sem=p_recv.at[source],
+            send_sem=pf_send.at[source], recv_sem=p_recv.at[source],
             device_id={"ctx": source * 2 + core}, device_id_type=MESH,
         )
 
     def f_copy(source):
         return pltpu.make_async_remote_copy(
             src_ref=chain.at[source, mine_rows], dst_ref=chain.at[source, mine_rows],
-            send_sem=f_send.at[source], recv_sem=f_recv.at[source],
+            send_sem=pf_send.at[source], recv_sem=f_recv.at[source],
             device_id={"ctx": peer}, device_id_type=MESH,
         )
 
@@ -274,28 +330,6 @@
         @pl.when(target > chip)
         def _():
             p_copy(target).start()
-
-    for o in range(NZ):
-
-        @pl.when(core == o % 2)
-        def _():
-            if o == 0:
-                w1_mine.wait()
-            else:
-                w1_copy(-o).wait_recv()
-
-    def w2_copy(d):
-        target = lax.rem(chip + d, CHIPS)
-        tiles = wo.at[half, :, pl.ds(row_tile, 16), pl.ds(col_tile, 128)]
-        return pltpu.make_async_remote_copy(
-            src_ref=tiles, dst_ref=tiles,
-            send_sem=w2_send.at[d], recv_sem=w2_recv.at[d],
-            device_id={"ctx": target * 2 + core}, device_id_type=MESH,
-        )
-
-    @pl.loop(1, CHIPS)
-    def _(d):
-        w2_copy(d).start()
 
     state[...] = jnp.zeros_like(state)
 
@@ -318,28 +352,11 @@
     entry = jnp.where(core == 0, entry, moved)
     att_own[...] = (local_s[...] + mm3(reader_s[...], entry)).astype(BF)
 
-    order_d, parent_d = TREE_D
-    d_copy, d_kids = tree_copies(order_d, parent_d, att_own, att, d_send, d_recv)
+    order_d, d_copy, d_kids = tree_copies(TREE_D, att_own, att, d_send, d_recv)
     for o in d_kids[0]:
         d_copy(o).start()
 
-    def w2_arrival(d):
-        source = lax.rem(chip + CHIPS - d, CHIPS)
-        tiles = wo.at[
-            half, :,
-            pl.ds(pl.multiple_of((source // 2) * 16, 16), 16),
-            pl.ds(pl.multiple_of(lax.rem(source, 2) * 128, 128), 128),
-        ]
-        return pltpu.make_async_remote_copy(
-            src_ref=tiles, dst_ref=tiles,
-            send_sem=w2_send.at[d], recv_sem=w2_recv.at[d],
-            device_id={"ctx": source * 2 + core}, device_id_type=MESH,
-        )
-
-    @pl.loop(1, CHIPS)
-    def _(d):
-        w2_arrival(d).wait_recv()
-
+    w2_bytes.wait_recv()
     w3_copy = pltpu.make_async_remote_copy(
         src_ref=wo.at[half], dst_ref=wo.at[half], send_sem=w3_send, recv_sem=w3_recv,
         device_id={"ctx": peer}, device_id_type=MESH,
@@ -360,16 +377,18 @@
         d_copy(o).wait_recv()
         for q in d_kids.get(o, ()):
             d_copy(q).start()
-        result = result + dot(att[o % NZ], columns(o))
+        if o != 8:
+            result = result + dot(att[o % NZ], columns(o))
     out[...] = result.astype(BF)
 
-    for o in order_a:
-        a_copy(o).wait_send()
-
-        @pl.when(core == o % 2)
-        def _():
-            w1_copy(o).wait_send()
-
+    bytes_of(tok.at[pl.ds(0, NZ - 1)], a_send, a_send).wait_send()
+    for k in range(2):
+
+        @pl.when(core == k)
+        def _():
+            w1_bytes(w1_counts[k]).wait_send()
+
+    w2_bytes.wait_send()
     c_copy.wait_send()
 
     @pl.loop(0, CHIPS)
@@ -382,26 +401,22 @@
         def _():
             f_copy(i).wait_send()
 
-        @pl.when(i > 0)
-        def _():
-            w2_copy(i).wait_send()
-
     w3_copy.wait_send()
-    for o in order_d:
-        d_copy(o).wait_send()
+    bytes_of(att.at[pl.ds(0, NZ - 1)], d_send, d_send).wait_send()
 
 
 def shards(tokens, w_query, w_key, w_value, w_beta, beta_bias, w_out):
     hbm = pl.BlockSpec(memory_space=pltpu.HBM)
     vmem = pl.BlockSpec(memory_space=pltpu.VMEM)
-    smem = pl.BlockSpec(memory_space=pltpu.SMEM)
     dma = pltpu.SemaphoreType.DMA
     return pl.pallas_call(
         kernel,
         out_shape=jax.ShapeDtypeStruct((ROWS, FEAT), BF),
-        in_specs=[hbm, hbm, hbm, hbm, vmem, smem, hbm],
+        in_specs=[hbm] * 7,
         out_specs=vmem,
         scratch_shapes=[
+            pltpu.VMEM((1, NZ * FEAT), BF),
+            pltpu.SMEM((1,), F32),
             pltpu.VMEM((ROWS, FEAT), BF),
             pltpu.VMEM((NZ, ROWS, FEAT), BF),
             pltpu.VMEM((NZ * FEAT, 3 * DK), BF),
@@ -418,10 +433,9 @@
             pltpu.VMEM((NZ, ROWS, DK), BF),
             pltpu.VMEM((ROWS, DK), F32),
             pltpu.VMEM((ROWS, DK), F32),
-            dma, dma((3,)), dma((NZ,)), dma((NZ,)),
-            dma((NZ,)), dma((NZ,)), dma, dma((CHIPS,)), dma((CHIPS,)), dma, dma,
-            dma, dma, dma((CHIPS,)), dma((CHIPS,)), dma((CHIPS,)), dma((CHIPS,)),
-            dma((NZ,)), dma((NZ,)), pltpu.SemaphoreType.REGULAR,
+            dma, dma((3,)), dma, dma((NZ,)), dma, dma, dma, dma, dma, dma, dma,
+            dma, dma, dma((CHIPS,)), dma((CHIPS,)), dma((CHIPS,)), dma, dma((NZ,)),
+            pltpu.SemaphoreType.REGULAR((3,)),
         ],
         compiler_params=pltpu.CompilerParams(
             collective_id=0, has_side_effects=True, vmem_limit_bytes=63 * 2**20

time: 72.2 us -> 68 us (0.942)
  Pallas kernels: 69.9 us -> 65.3 us
    pallas_call x1, Pallas kernels: 69.9 us -> 65.3 us  [shards(): pl.pallas_call(kernel, out_shape=jax.ShapeDtypeStruct((ROWS, FEAT), BF),...]
where the time goes in v2:
time: 68 us; the launch traced here: 67.5 us
  Pallas kernels  65.3 us (96%)
  local copies, waits for them, and re-layouts  1.47 us (2%)
    pallas_call x1, Pallas kernels, shards(): pl.pallas_call(kernel, out_shape=jax.ShapeDtypeStruct((ROWS, FEAT), BF),...  65.3 us
    unnamed x1, local copies, waits for them, and re-layouts  1.47 us

profile of v2, /device:TPU:6, one launch (start us, length us, event | category | flops | bytes accessed | tf_op | source)
XLA Modules:
  0.0 67.5 jit_solution(3184128153251965406)
XLA Ops:
  0.7 65.3 %shard_map.73 = bf16[128,256]{1,0:T(8,128)(2,1)} custom-call(bf16[128,256]{1,0:T(8,128)(2,1)} %tokens.1, bf16[4096,128]{1,0:T(8,128)(2,1)} %w_query.1, bf16[4096,128]{1,0:T(8,128)(2,1)} %w_key.1, bf16[4096,128]{1,0:T(8,128)(2,1)} %w_value.1, bf16[1,4096]{1,0:T(2,128)(2,1)} %bitcast.1, f32[1]{0:T(128)S(6)} %copy.9.bias_in, bf16[128,4096]{1,0:T(8,128)(2,1)} %w_out.1), custom_call_target="tpu_custom_call" | custom-call | tf_op jit(solution)/shard_map/pallas_call | solution.py:412
  66.0 1.5 %copy.10 = bf16[128,256]{1,0:T(8,128)(2,1)} copy(bf16[128,256]{1,0:T(8,128)(2,1)} %shard_map.73) | data formatting | bytes 131072

commit v3 on v2

--- a/solution.py
+++ b/solution.py
@@ -17,7 +17,7 @@
 ROWS = 128
 FEAT = 256
 DK = 128
-LAG = 4
+LAG = 8
 W1_AT = 1
 W2_AT = 10
 
@@ -305,27 +305,27 @@
     def p_copy(target):
         return pltpu.make_async_remote_copy(
             src_ref=total.at[mine_rows], dst_ref=chain.at[chip, mine_rows],
-            send_sem=pf_send.at[target], recv_sem=p_recv.at[chip],
+            send_sem=pf_send.at[0], recv_sem=p_recv.at[chip],
             device_id={"ctx": target * 2 + core}, device_id_type=MESH,
         )
 
     def p_arrival(source):
         return pltpu.make_async_remote_copy(
             src_ref=total.at[mine_rows], dst_ref=chain.at[source, mine_rows],
-            send_sem=pf_send.at[source], recv_sem=p_recv.at[source],
+            send_sem=pf_send.at[0], recv_sem=p_recv.at[source],
             device_id={"ctx": source * 2 + core}, device_id_type=MESH,
         )
 
     def f_copy(source):
         return pltpu.make_async_remote_copy(
             src_ref=chain.at[source, mine_rows], dst_ref=chain.at[source, mine_rows],
-            send_sem=pf_send.at[source], recv_sem=f_recv.at[source],
+            send_sem=pf_send.at[1], recv_sem=f_recv.at[source],
             device_id={"ctx": peer}, device_id_type=MESH,
         )
 
-    @pl.loop(0, CHIPS - 1)
+    @pl.loop(0, CHIPS)
     def _(i):
-        target = CHIPS - 1 - i
+        target = (XS - 1 - i // YS) * YS + lax.rem(y + 6 - lax.rem(i, YS), YS)
 
         @pl.when(target > chip)
         def _():
@@ -367,6 +367,29 @@
         device_id={"ctx": peer}, device_id_type=MESH,
     )
     w3_arrival.wait_recv()
+
+    bytes_of(tok.at[pl.ds(0, NZ - 1)], a_send, a_send).wait_send()
+    for k in range(2):
+
+        @pl.when(core == k)
+        def _():
+            w1_bytes(w1_counts[k]).wait_send()
+
+    w2_bytes.wait_send()
+    c_copy.wait_send()
+
+    def chain_bytes(count, send):
+        return bytes_of(chain.at[pl.ds(0, count), pl.ds(0, ROWS // 2)], send, send)
+
+    for i in range(CHIPS):
+
+        @pl.when(chip == i)
+        def _():
+            if i < CHIPS - 1:
+                chain_bytes(CHIPS - 1 - i, pf_send.at[0]).wait_send()
+            if i > 0:
+                chain_bytes(i, pf_send.at[1]).wait_send()
+
 
     def columns(off):
         owner = head_at(-off)
@@ -380,26 +403,6 @@
         if o != 8:
             result = result + dot(att[o % NZ], columns(o))
     out[...] = result.astype(BF)
-
-    bytes_of(tok.at[pl.ds(0, NZ - 1)], a_send, a_send).wait_send()
-    for k in range(2):
-
-        @pl.when(core == k)
-        def _():
-            w1_bytes(w1_counts[k]).wait_send()
-
-    w2_bytes.wait_send()
-    c_copy.wait_send()
-
-    @pl.loop(0, CHIPS)
-    def _(i):
-        @pl.when(i > chip)
-        def _():
-            p_copy(i).wait_send()
-
-        @pl.when(i < chip)
-        def _():
-            f_copy(i).wait_send()
 
     w3_copy.wait_send()
     bytes_of(att.at[pl.ds(0, NZ - 1)], d_send, d_send).wait_send()
@@ -434,7 +437,7 @@
             pltpu.VMEM((ROWS, DK), F32),
             pltpu.VMEM((ROWS, DK), F32),
             dma, dma((3,)), dma, dma((NZ,)), dma, dma, dma, dma, dma, dma, dma,
-            dma, dma, dma((CHIPS,)), dma((CHIPS,)), dma((CHIPS,)), dma, dma((NZ,)),
+            dma, dma, dma((2,)), dma((CHIPS,)), dma((CHIPS,)), dma, dma((NZ,)),
             pltpu.SemaphoreType.REGULAR((3,)),
         ],
         compiler_params=pltpu.CompilerParams(

time: 68 us -> 66.5 us (0.978)
  Pallas kernels: 65.3 us -> 63.7 us
    pallas_call x1, Pallas kernels: 65.3 us -> 63.7 us  [shards(): pl.pallas_call(kernel, out_shape=jax.ShapeDtypeStruct((ROWS, FEAT), BF),...]
where the time goes in v3:
time: 66.5 us; the launch traced here: 65.8 us
  Pallas kernels  63.7 us (96%)
  local copies, waits for them, and re-layouts  1.47 us (2%)
    pallas_call x1, Pallas kernels, shards(): pl.pallas_call(kernel, out_shape=jax.ShapeDtypeStruct((ROWS, FEAT), BF),...  63.7 us
    unnamed x1, local copies, waits for them, and re-layouts  1.47 us

profile of v3, /device:TPU:6, one launch (start us, length us, event | category | flops | bytes accessed | tf_op | source)
XLA Modules:
  0.0 65.8 jit_solution(16748295881651173257)
XLA Ops:
  0.7 63.7 %shard_map.73 = bf16[128,256]{1,0:T(8,128)(2,1)} custom-call(bf16[128,256]{1,0:T(8,128)(2,1)} %tokens.1, bf16[4096,128]{1,0:T(8,128)(2,1)} %w_query.1, bf16[4096,128]{1,0:T(8,128)(2,1)} %w_key.1, bf16[4096,128]{1,0:T(8,128)(2,1)} %w_value.1, bf16[1,4096]{1,0:T(2,128)(2,1)} %bitcast.1, f32[1]{0:T(128)S(6)} %copy.9.bias_in, bf16[128,4096]{1,0:T(8,128)(2,1)} %w_out.1), custom_call_target="tpu_custom_call" | custom-call | tf_op jit(solution)/shard_map/pallas_call | solution.py:415
  64.4 1.5 %copy.10 = bf16[128,256]{1,0:T(8,128)(2,1)} copy(bf16[128,256]{1,0:T(8,128)(2,1)} %shard_map.73) | data formatting | bytes 131072

commit v4 on v3

--- a/solution.py
+++ b/solution.py
@@ -37,7 +37,8 @@
             parent[s] = 0
         for e in (1, -1, 2, -2):
             parent[s + e] = s
-    return [5, -5, 1, -1, 2, -2, 4, -4, 6, -6, 3, -3, 7, -7, 8, -8], parent
+    parent.update({3: 2, -3: -2})
+    return [5, -5, 2, -2, 1, -1, 3, -3, 7, -7, 4, -4, 6, -6, 8, -8], parent
 
 
 TREE_A = tree_step2()

time: 66.5 us -> 65.9 us (level)
  Pallas kernels: 63.7 us -> 62.7 us
    pallas_call x1, Pallas kernels: 63.7 us -> 62.7 us  [shards(): pl.pallas_call(kernel, out_shape=jax.ShapeDtypeStruct((ROWS, FEAT), BF),...]
where the time goes in v4:
time: 65.9 us; the launch traced here: 64.8 us
  Pallas kernels  62.7 us (95%)
  local copies, waits for them, and re-layouts  1.47 us (2%)
  between operations  0.66 us (1%)
    pallas_call x1, Pallas kernels, shards(): pl.pallas_call(kernel, out_shape=jax.ShapeDtypeStruct((ROWS, FEAT), BF),...  62.7 us
    unnamed x1, local copies, waits for them, and re-layouts  1.47 us

profile of v4, /device:TPU:6, one launch (start us, length us, event | category | flops | bytes accessed | tf_op | source)
XLA Modules:
  0.0 64.8 jit_solution(4930042719588936585)
XLA Ops:
  0.7 62.7 %shard_map.73 = bf16[128,256]{1,0:T(8,128)(2,1)} custom-call(bf16[128,256]{1,0:T(8,128)(2,1)} %tokens.1, bf16[4096,128]{1,0:T(8,128)(2,1)} %w_query.1, bf16[4096,128]{1,0:T(8,128)(2,1)} %w_key.1, bf16[4096,128]{1,0:T(8,128)(2,1)} %w_value.1, bf16[1,4096]{1,0:T(2,128)(2,1)} %bitcast.1, f32[1]{0:T(128)S(6)} %copy.9.bias_in, bf16[128,4096]{1,0:T(8,128)(2,1)} %w_out.1), custom_call_target="tpu_custom_call" | custom-call | tf_op jit(solution)/shard_map/pallas_call | solution.py:416
  63.4 1.5 %copy.10 = bf16[128,256]{1,0:T(8,128)(2,1)} copy(bf16[128,256]{1,0:T(8,128)(2,1)} %shard_map.73) | data formatting | bytes 131072

commit v5 on v4

--- a/solution.py
+++ b/solution.py
@@ -19,7 +19,7 @@
 DK = 128
 LAG = 8
 W1_AT = 1
-W2_AT = 10
+W2_AT = 12
 
 
 def tree_step2():
@@ -27,7 +27,7 @@
     for s in (1, -1):
         parent.update({2 * s: 0, 4 * s: 2 * s, 6 * s: 4 * s, 8 * s: 6 * s})
         parent.update({s: 0, 3 * s: 2 * s, 5 * s: 4 * s, 7 * s: 6 * s})
-    return [2, -2, 1, -1, 4, -4, 3, -3, 6, -6, 5, -5, 8, -8, 7, -7], parent
+    return [2, -2, 4, -4, 1, -1, 6, -6, 3, -3, 8, -8, 5, -5, 7, -7], parent
 
 
 def tree_seed5():

time: 65.9 us -> 66.3 us (level)
  no operation moved by 1% of the time
where the time goes in v5:
time: 66.3 us; the launch traced here: 65.2 us
  Pallas kernels  63.1 us (95%)
  local copies, waits for them, and re-layouts  1.47 us (2%)
    pallas_call x1, Pallas kernels, shards(): pl.pallas_call(kernel, out_shape=jax.ShapeDtypeStruct((ROWS, FEAT), BF),...  63.1 us
    unnamed x1, local copies, waits for them, and re-layouts  1.47 us

profile of v5, /device:TPU:6, one launch (start us, length us, event | category | flops | bytes accessed | tf_op | source)
XLA Modules:
  0.0 65.2 jit_solution(15064420425464824391)
XLA Ops:
  0.7 63.1 %shard_map.73 = bf16[128,256]{1,0:T(8,128)(2,1)} custom-call(bf16[128,256]{1,0:T(8,128)(2,1)} %tokens.1, bf16[4096,128]{1,0:T(8,128)(2,1)} %w_query.1, bf16[4096,128]{1,0:T(8,128)(2,1)} %w_key.1, bf16[4096,128]{1,0:T(8,128)(2,1)} %w_value.1, bf16[1,4096]{1,0:T(2,128)(2,1)} %bitcast.1, f32[1]{0:T(128)S(6)} %copy.9.bias_in, bf16[128,4096]{1,0:T(8,128)(2,1)} %w_out.1), custom_call_target="tpu_custom_call" | custom-call | tf_op jit(solution)/shard_map/pallas_call | solution.py:416
  63.7 1.5 %copy.10 = bf16[128,256]{1,0:T(8,128)(2,1)} copy(bf16[128,256]{1,0:T(8,128)(2,1)} %shard_map.73) | data formatting | bytes 131072
